TPU v7x, 32 devices: a whole 2x2x4 slice. The times are simulated.
32 devices in a mesh: gx: 4 (over x, core), gy: 4 (over z), ta: 2 (over y).
Axes of the slice: x: 2, y: 2, z: 4, core: 2. Of those that a mesh axis runs over, the one named last changes fastest.
Arguments:
- tokens: bfloat16 [4, 4, 4, 128, 512], P('gx', 'gy', 'ta'), may hold values from -6 to 6
- validity: int32 [4, 4, 4, 128], P('gx', 'gy', 'ta'), may hold values 0 or 1
- tile_counts: int32 [4, 4], replicated, may hold values from 16 to 128, as said below
- neighbours: int32 [4, 4, 9], P('gx', 'gy'), may hold values from 0 to 1, as said below
- mask_token: bfloat16 [512], replicated, may hold values from -4 to 4
- norm_gains: float32 [3, 512], replicated, may hold values from 0.25 to 1.75
- agent_qkv: bfloat16 [512, 1536], replicated, may hold values from -3 to 3
- agent_out: bfloat16 [512, 512], replicated, may hold values from -0.25 to 0.25
- time_qkv: bfloat16 [512, 1536], replicated, may hold values from -3 to 3
- time_out: bfloat16 [512, 512], replicated, may hold values from -0.25 to 0.25
- widen_weight: bfloat16 [512, 2048], replicated, may hold values from -0.25 to 0.25
- narrow_weight: bfloat16 [2048, 512], replicated, may hold values from -0.125 to 0.125
Outputs:
- layer_out: bfloat16 [4, 4, 4, 128, 512], P('gx', 'gy', 'ta')
Inputs may be any that keep to these rules, and one draw needn't show every extreme that they name: Tile i, j has its live agents in slots 0 to tile_counts[i, j] - 1; some tile is full. `neighbours`: entry 3 (di + 1) + (dj + 1) is 1 when the tile attends to the tile at offset di, dj; the centre entry is always 1. `validity`: 1 marks an observed agent step.
All inputs are finite; a program needn't handle non-finite values. No bound on the sum of `validity` on one device may be relied on, other than what follows from the above.
Results may differ from a plain program's by a relative error of at most 0.015.
Values may be sent and summed in bfloat16 or wider, within the bound.
A program may use at most 128 MiB of HBM per device.

v0:
```python
import math

import jax
import jax.numpy as jnp
from jax import lax
from jax.sharding import PartitionSpec as P

HEADS = 8


EPSILON = 1e-05
NEGATIVE = -1e30


def extended(array, sides, width):
    for axis, dim in sides:
        count, length = (lax.axis_size(axis), array.shape[dim])
        up = [(i, (i + 1) % count) for i in range(count - 1)]
        down = [(j, i) for i, j in up]
        last = lax.slice_in_dim(array, length - width, length, axis=dim)
        first = lax.slice_in_dim(array, 0, width, axis=dim)
        before = lax.ppermute(last, axis, up)
        after = lax.ppermute(first, axis, down)
        array = jnp.concatenate([before, array, after], axis=dim)
    return array


def layer_norm(values, gain_row):
    values = values.astype(jnp.float32)
    center = values - jnp.mean(values, axis=-1, keepdims=True)
    spread = jnp.mean(center * center, axis=-1, keepdims=True)
    return (center * lax.rsqrt(spread + EPSILON) * gain_row).astype(jnp.bfloat16)


def project(values, weight):
    return jnp.dot(values, weight, preferred_element_type=jnp.float32)


def agent_block(own_rows, beside_all, key_live, head_count):
    slot_count = own_rows.shape[0]
    model_width = own_rows.shape[1]
    head_dim = model_width // head_count
    own_queries = own_rows.reshape(slot_count, head_count, head_dim)
    key_rows = beside_all[..., :model_width].reshape(3, 3, slot_count, head_count, head_dim)
    value_rows = beside_all[..., model_width:].reshape(9 * slot_count, head_count, head_dim)
    scores = jnp.einsum(
        "qhd,xykhd->hqxyk", own_queries, key_rows, preferred_element_type=jnp.float32
    )
    scores = scores.reshape(head_count, slot_count, 9 * slot_count) * (1.0 / math.sqrt(head_dim))
    scores = jnp.where(key_live, scores, NEGATIVE)
    row_max = jnp.max(scores, axis=-1, keepdims=True)
    weights = jnp.exp(scores - row_max)
    weights = (weights / jnp.sum(weights, axis=-1, keepdims=True)).astype(jnp.bfloat16)
    attended = jnp.einsum("hqn,nhd->qhd", weights, value_rows, preferred_element_type=jnp.float32)
    return attended.reshape(slot_count, model_width).astype(jnp.bfloat16)


def time_block(exchanged, head_count):
    step_count = exchanged.shape[0]
    slot_count = exchanged.shape[1]
    model_width = exchanged.shape[2] // 3
    head_dim = model_width // head_count
    own_queries = exchanged[..., :model_width].reshape(step_count, slot_count, head_count, head_dim)
    key_rows = exchanged[..., model_width : 2 * model_width].reshape(
        step_count, slot_count, head_count, head_dim
    )
    value_rows = (
        exchanged[..., 2 * model_width :]
        .astype(jnp.float32)
        .reshape(step_count, slot_count, head_count, head_dim)
    )
    scores = jnp.einsum(
        "qahd,kahd->ahqk", own_queries, key_rows, preferred_element_type=jnp.float32
    )
    scores = scores * (1.0 / math.sqrt(head_dim))
    row_max = jnp.max(scores, axis=-1, keepdims=True)
    weights = jnp.exp(scores - row_max)
    weights = weights / jnp.sum(weights, axis=-1, keepdims=True)
    attended = jnp.einsum("ahqk,kahd->qahd", weights, value_rows, precision=lax.Precision.HIGHEST)
    return attended.reshape(step_count, slot_count, model_width).astype(jnp.bfloat16)


def per_device(
    tokens,
    validity,
    tile_counts,
    neighbours,
    mask_token,
    norm_gains,
    agent_qkv,
    agent_out,
    time_qkv,
    time_out,
    widen_weight,
    narrow_weight,
):
    model_width = tokens.shape[-1]
    head_count = HEADS
    moments = tokens.shape[2]
    slot_count = tokens.shape[3]
    masked_input = jnp.where(validity[..., None] == 1, tokens, mask_token)
    normed = layer_norm(masked_input, norm_gains[0])
    packed = project(normed, agent_qkv).astype(jnp.bfloat16)
    queries = packed[..., :model_width]
    beside_all = extended(packed[..., model_width:], (("gx", 0), ("gy", 1)), 1)
    column_index = lax.axis_index("gx")
    row_index = lax.axis_index("gy")
    padded_counts = jnp.pad(tile_counts, 1)
    near_counts = lax.dynamic_slice(padded_counts, (column_index, row_index), (3, 3))
    chosen = neighbours[0, 0].reshape(3, 3) == 1
    slot_ids = jnp.arange(slot_count, dtype=jnp.int32)
    key_live = ((slot_ids[None, None, :] < near_counts[:, :, None]) & chosen[:, :, None]).reshape(
        9 * slot_count
    )
    attended = jnp.stack(
        [
            agent_block(queries[0, 0, moment], beside_all[:, :, moment], key_live, head_count)
            for moment in range(moments)
        ]
    )[None, None]
    after_agents = (masked_input.astype(jnp.float32) + project(attended, agent_out)).astype(
        jnp.bfloat16
    )
    normed = layer_norm(after_agents, norm_gains[1])
    packed = project(normed, time_qkv).astype(jnp.bfloat16)
    share_count = lax.axis_size("ta")
    share_slots = slot_count // share_count
    grouped = packed.reshape(1, 1, moments, share_count, share_slots, 3 * model_width)
    spread_rows = time_block(
        lax.all_to_all(grouped, "ta", split_axis=3, concat_axis=2, tiled=True)[0, 0, :, 0],
        head_count,
    )[None, None, :, None]
    returned = lax.all_to_all(spread_rows, "ta", split_axis=2, concat_axis=3, tiled=True)
    attended = returned.reshape(1, 1, moments, slot_count, model_width)
    after_time = (after_agents.astype(jnp.float32) + project(attended, time_out)).astype(
        jnp.bfloat16
    )
    normed = layer_norm(after_time, norm_gains[2])
    hidden = jnp.maximum(project(normed, widen_weight), 0.0).astype(jnp.bfloat16)
    return (after_time.astype(jnp.float32) + project(hidden, narrow_weight)).astype(jnp.bfloat16)


def solution(mesh):
    in_specs = (
        P("gx", "gy", "ta", None, None),
        P("gx", "gy", "ta", None),
        P(),
        P("gx", "gy", None),
        P(),
        P(),
        P(),
        P(),
        P(),
        P(),
        P(),
        P(),
    )
    out_specs = P("gx", "gy", "ta", None, None)
    return jax.shard_map(
        per_device, mesh=mesh, in_specs=in_specs, out_specs=out_specs, check_vma=False
    )
```

profile of v0, /device:TPU:1, one launch (start us, length us, event | category | flops | bytes accessed | tf_op | source)
XLA Modules:
  0.0 148.7 jit_solution(17013513402019384789)
XLA Ops:
  0.0 0.8 compare_bitcast_fusion
  0.8 1.2 convert_reduce_fusion
  2.0 1.2 fusion.36
  3.2 1.4 fusion.78
  4.6 2.2 %fusion.1 = bf16[1,1,2,128,1536]{4,3,2,1,0:T(8,128)(2,1)S(1)} fusion(bf16[512,1536]{1,0:T(8,128)(2,1)} %param.18, f32[512]{0:T(512)S(1)} %bitcast.134, f32[2,128]{1,0:T(2,128)S(1)} %add_rsqrt_fusion.2, f32[2,128]{1,0:T(2,128)S(1)} %broadcast_multiply_fusion.4, bf16[1,1,2,128,512]{4,3,2,1,0:T(8,128)(2,1)} %param.12, ...), kind=kOutput, calls=%fused_computation.11 | convolution fusion | flops 403832832 | bytes 2626816 | tf_op jit(solution)/shard_map/dot_general | solution.py:36
  6.9 4.6 %collective-permute-start = (bf16[1,1,2,128,1024]{4,3,2,1,0:T(8,128)(2,1)S(1)}, bf16[1,1,2,128,1024]{4,3,2,1,0:T(8,128)(2,1)S(1)}, u32[]{:S(2)}, u32[]{:S(2)}) collective-permute-start(bf16[1,1,2,128,1024]{4,3,2,1,0:T(8,128)(2,1)S(1)} %slice.63), channel_id=1, source_target_pairs={{0,8},{8,16},{16,24},{1,9},{9,17},{17,25},{2,10},{10,18},{18,26},{... | collective-permute-start | bytes 1572872 | tf_op jit(solution)/shard_map/ppermute | solution.py:22
  11.6 1.9 %collective-permute-start.1 = (bf16[1,1,2,128,1024]{4,3,2,1,0:T(8,128)(2,1)S(1)}, bf16[1,1,2,128,1024]{4,3,2,1,0:T(8,128)(2,1)S(1)}, u32[]{:S(2)}, u32[]{:S(2)}) collective-permute-start(bf16[1,1,2,128,1024]{4,3,2,1,0:T(8,128)(2,1)S(1)} %slice.63), channel_id=1, source_target_pairs={{8,0},{16,8},{24,16},{9,1},{17,9},{25,17},{10,2},{18,10},{26,18},{... | collective-permute-start | bytes 1572872 | tf_op jit(solution)/shard_map/ppermute | solution.py:23
  13.5 4.2 %collective-permute-done = bf16[1,1,2,128,1024]{4,3,2,1,0:T(8,128)(2,1)S(1)} collective-permute-done((bf16[1,1,2,128,1024]{4,3,2,1,0:T(8,128)(2,1)S(1)}, bf16[1,1,2,128,1024]{4,3,2,1,0:T(8,128)(2,1)S(1)}, u32[]{:S(2)}, u32[]{:S(2)}) %collective-permute-start) | collective-permute-done | bytes 524320 | tf_op jit(solution)/shard_map/ppermute | solution.py:22
  17.7 4.4 %collective-permute-done.1 = bf16[1,1,2,128,1024]{4,3,2,1,0:T(8,128)(2,1)S(1)} collective-permute-done((bf16[1,1,2,128,1024]{4,3,2,1,0:T(8,128)(2,1)S(1)}, bf16[1,1,2,128,1024]{4,3,2,1,0:T(8,128)(2,1)S(1)}, u32[]{:S(2)}, u32[]{:S(2)}) %collective-permute-start.1) | collective-permute-done | bytes 524320 | tf_op jit(solution)/shard_map/ppermute | solution.py:23
  22.1 0.8 copy-done.3
  22.9 1.3 pad_maximum_fusion.1
  24.2 4.3 %collective-permute-start.2 = (bf16[3,1,2,128,1024]{4,3,2,1,0:T(8,128)(2,1)}, bf16[3,1,2,128,1024]{4,3,2,1,0:T(8,128)(2,1)}, u32[]{:S(2)}, u32[]{:S(2)}) collective-permute-start(bf16[3,1,2,128,1024]{4,3,2,1,0:T(8,128)(2,1)} %pad_maximum_fusion.1), channel_id=1, source_target_pairs={{0,2},{2,4},{4,6},{1,3},{3,5},{5,7},{8,10},{10,12},{12,14},{9,11},... | collective-permute-start | bytes 4718600 | tf_op jit(solution)/shard_map/ppermute | solution.py:22
  28.5 1.3 collective-permute-start.3
  30.0 1.0 fusion.77
  31.4 0.6 and.17
  32.0 23.7 %collective-permute-done.2 = bf16[3,1,2,128,1024]{4,3,2,1,0:T(8,128)(2,1)} collective-permute-done((bf16[3,1,2,128,1024]{4,3,2,1,0:T(8,128)(2,1)}, bf16[3,1,2,128,1024]{4,3,2,1,0:T(8,128)(2,1)}, u32[]{:S(2)}, u32[]{:S(2)}) %collective-permute-start.2) | collective-permute-done | bytes 1572896 | tf_op jit(solution)/shard_map/ppermute | solution.py:22
  55.7 5.2 %collective-permute-done.3 = bf16[3,1,2,128,1024]{4,3,2,1,0:T(8,128)(2,1)} collective-permute-done((bf16[3,1,2,128,1024]{4,3,2,1,0:T(8,128)(2,1)}, bf16[3,1,2,128,1024]{4,3,2,1,0:T(8,128)(2,1)}, u32[]{:S(2)}, u32[]{:S(2)}) %collective-permute-start.3) | collective-permute-done | bytes 1572896 | tf_op jit(solution)/shard_map/ppermute | solution.py:23
  60.9 2.3 %pad_maximum_fusion = bf16[3,3,2,128,1024]{4,3,2,1,0:T(8,128)(2,1)S(1)} fusion(bf16[3,1,2,128,1024]{4,3,2,1,0:T(8,128)(2,1)} %collective-permute-done.3, bf16[1,1,2,128,1024]{4,3,2,1,0:T(8,128)(2,1)} %copy-done.3, bf16[1,1,2,128,1024]{4,3,2,1,0:T(8,128)(2,1)S(1)} %slice.63, bf16[1,1,2,128,1024]{4,3,2,1,0:T(8,128)(2,1)S(1)} %collective-permute-done, ...), kind=kLoop, calls=%fused_computation | loop fusion | flops 9437184 | bytes 9437184 | tf_op jit(solution)/shard_map/concatenate | solution.py:24
  63.2 0.7 slice_bitcast_fusion.1
  63.9 1.9 %fusion.74 = (bf16[3,3,128,512]{3,2,1,0:T(8,128)(2,1)}, bf16[3,3,128,512]{3,2,1,0:T(8,128)(2,1)}, bf16[3,3,128,512]{3,2,1,0:T(8,128)(2,1)}, bf16[3,3,128,512]{3,2,1,0:T(8,128)(2,1)S(1)}) fusion(bf16[3,3,128,1024]{3,2,1,0:T(8,128)(2,1)S(1)} %get-tuple-element.7, bf16[3,3,128,1024]{3,2,1,0:T(8,128)(2,1)S(1)} %get-tuple-element.8), kind=kLoop, calls=%fused_computation.96 | loop fusion | bytes 9437184 | tf_op jit(solution)/shard_map/slice | solution.py:45
  65.8 2.4 %copy.45 = bf16[3,3,128,512]{2,3,1,0:T(8,128)(2,1)} copy(bf16[3,3,128,512]{3,2,1,0:T(8,128)(2,1)} %get-tuple-element.10) | data formatting | bytes 2359296 | tf_op jit(solution)/shard_map/slice | solution.py:44
  68.2 1.4 copy.50
  69.6 4.7 %select_reduce_fusion.1 = (f32[8,128]{1,0:T(8,128)S(1)}, f32[8,128,3,3,128]{1,4,3,2,0:T(8,128)}) fusion(pred[3,3,128]{2,1,0:T(4,128)(4,1)S(1)} %fusion.69, bf16[128,8,64,1,1]{0,2,4,3,1:T(8,128)(2,1)S(1)} %bitcast.128, bf16[3,3,128,8,64]{2,4,3,1,0:T(8,128)(2,1)} %bitcast.121), kind=kOutput, calls=%fused_computation.6 | convolution fusion | flops 154532864 | bytes 6034560 | tf_op jit(solution)/shard_map/qhd,xykhd->hqxyk/dot_general | solution.py:46
  74.3 6.3 %copy.47 = f32[8,128,1152]{2,1,0:T(8,128)} copy(f32[8,128,1152]{1,2,0:T(8,128)} %bitcast.117) | data formatting | bytes 9437184 | tf_op jit(solution)/shard_map/mul | solution.py:49
  80.6 2.3 %copy.43 = bf16[3,3,128,512]{2,1,0,3:T(4,128)(2,1)} copy(bf16[3,3,128,512]{3,2,1,0:T(8,128)(2,1)S(1)} %copy-done.2) | data formatting | bytes 2359296 | tf_op jit(solution)/shard_map/slice | solution.py:45
  82.9 4.0 %reshape.208 = bf16[1152,8,64]{0,2,1:T(8,128)(2,1)} reshape(bf16[3,3,128,512]{2,1,0,3:T(4,128)(2,1)} %copy.43) | data formatting | bytes 2359296 | tf_op jit(solution)/shard_map/reshape | solution.py:45
  86.9 7.0 %exponential_reduce_fusion.1 = (f32[8,128]{1,0:T(8,128)S(1)}, f32[8,128]{1,0:T(8,128)S(1)}, f32[8,128,3,3,128]{1,4,3,2,0:T(8,128)}) fusion(f32[8,128,3,3,128]{1,4,3,2,0:T(8,128)} %get-tuple-element.22, f32[8,128]{1,0:T(8,128)S(1)} %get-tuple-element.21, pred[3,3,128]{2,1,0:T(4,128)(4,1)S(1)} %fusion.69, bf16[128,8,64,1,1]{0,2,4,3,1:T(8,128)(2,1)S(1)} %bitcast.129, ...), kind=kOutput, calls=%fused_computation.4 | convolution fusion | flops 158070784 | bytes 10761344 | tf_op jit(solution)/shard_map/qhd,xykhd->hqxyk/dot_general | solution.py:46
  93.9 1.5 %fusion.28 = bf16[8,64,128]{2,1,0:T(8,128)(2,1)S(1)} fusion(bf16[1152,8,64]{0,2,1:T(8,128)(2,1)S(1)} %copy-done.5, f32[8,128,1152]{2,1,0:T(8,128)S(1)} %bitcast.120, f32[8,128]{1,0:T(8,128)S(1)} %get-tuple-element.5, f32[8,128]{1,0:T(8,128)S(1)} %get-tuple-element.21, pred[1152]{0:T(1024)(128)(4,1)S(1)} %copy-done.10), kind=kOutput, calls=%fused_computation.41 | convolution fusion | flops 155779072 | bytes 6038656 | tf_op jit(solution)/shard_map/hqn,nhd->qhd/dot_general | solution.py:54
  95.5 0.8 copy.53
  96.3 3.2 %exponential_reduce_fusion = f32[8,128]{1,0:T(8,128)S(1)} fusion(f32[8,128,3,3,128]{1,4,3,2,0:T(8,128)} %get-tuple-element.23, f32[8,128]{1,0:T(8,128)S(1)} %get-tuple-element.6, pred[3,3,128]{2,1,0:T(4,128)(4,1)S(1)} %fusion.69), kind=kLoop, calls=%fused_computation.2 | loop fusion | flops 3537920 | bytes 4727936 | tf_op jit(solution)/shard_map/reduce_sum | solution.py:53
  99.5 6.2 %copy.52 = f32[8,128,1152]{2,1,0:T(8,128)} copy(f32[8,128,1152]{1,2,0:T(8,128)} %bitcast.118) | data formatting | bytes 9437184 | tf_op jit(solution)/shard_map/mul | solution.py:49
  105.7 2.3 %copy.48 = bf16[3,3,128,512]{2,1,0,3:T(4,128)(2,1)} copy(bf16[3,3,128,512]{3,2,1,0:T(8,128)(2,1)S(1)} %copy-done.1) | data formatting | bytes 2359296 | tf_op jit(solution)/shard_map/slice | solution.py:45
  108.0 2.8 %reshape.210 = bf16[1152,8,64]{0,2,1:T(8,128)(2,1)S(1)} reshape(bf16[3,3,128,512]{2,1,0,3:T(4,128)(2,1)} %copy.48) | data formatting | bytes 2359296 | tf_op jit(solution)/shard_map/reshape | solution.py:45
  110.9 4.3 %fusion.27 = bf16[8,64,128]{2,1,0:T(8,128)(2,1)} fusion(bf16[1152,8,64]{0,2,1:T(8,128)(2,1)S(1)} %reshape.210, f32[8,128,1152]{2,1,0:T(8,128)} %copy.52, f32[8,128]{1,0:T(8,128)S(1)} %exponential_reduce_fusion, f32[8,128]{1,0:T(8,128)S(1)} %get-tuple-element.6, pred[1152]{0:T(1024)(128)(4,1)} %and.17), kind=kOutput, calls=%fused_computation.40 | convolution fusion | flops 155779072 | bytes 6038656 | tf_op jit(solution)/shard_map/hqn,nhd->qhd/dot_general | solution.py:54
  115.2 1.0 copy.54
  116.2 1.6 %fusion.79 = (f32[2,128]{1,0:T(2,128)S(1)}, f32[1,1,2,128,512]{4,3,2,1,0:T(8,128)S(1)}) fusion(bf16[512,512]{1,0:T(8,128)(2,1)} %param.19, bf16[1,128,512]{2,1,0:T(8,128)(2,1)S(1)} %copy.54, bf16[1,128,512]{2,1,0:T(8,128)(2,1)} %copy.53, bf16[1,1,2,128,512]{4,3,2,1,0:T(8,128)(2,1)S(1)} %copy-done.6, bf16[512]{0:T(512)(128)(2,1)S(1)} %copy-done.8, ...), kind=kOutput, calls=%fused_computation.101 | convolution fusion | flops 135134976 | bytes 1575168 | tf_op jit(solution)/shard_map/dot_general | solution.py:36
  118.0 0.6 convolution_convert_fusion
  118.7 9.3 %all_to_all.30 = bf16[1,1,2,2,64,1536]{5,4,2,1,0,3:T(8,128)(2,1)S(1)} all-to-all(bf16[1,1,2,2,64,1536]{5,4,2,1,0,3:T(8,128)(2,1)S(1)} %copy.55), channel_id=1, replica_groups=mesh['gx'=4,'gy'=4,'ta'=2] {'ta'}, dimensions={3} | all-to-all | bytes 1572864 | tf_op jit(solution)/shard_map/all_to_all | solution.py:130
  128.1 1.1 reshape.215
  129.2 1.1 reshape.216
  130.2 0.3 reshape.214
  130.5 2.4 %fusion.80 = (f32[64,8,4]{2,1,0:T(8,128)S(1)}, f32[64,8,4,4]{2,3,1,0:T(4,128)S(1)}) fusion(bf16[4,64,8,64]{3,2,1,0:T(8,128)(2,1)} %reshape.216, bf16[4,64,8,64]{3,2,1,0:T(8,128)(2,1)} %reshape.215), kind=kOutput, calls=%fused_computation.102 | convolution fusion | flops 1062912 | bytes 565248 | tf_op jit(solution)/shard_map/qahd,kahd->ahqk/dot_general | solution.py:72
  133.0 1.0 fusion.33
  134.0 2.6 %fusion.9 = bf16[4,64,8,64]{3,0,2,1:T(4,128)(2,1)S(1)} fusion(f32[64,8,4,4]{2,3,1,0:T(4,128)S(1)} %get-tuple-element.27, bf16[4,64,8,64]{3,2,1,0:T(8,128)(2,1)S(1)} %reshape.214, f32[64,8,4]{2,1,0:T(8,128)S(1)} %fusion.33, f32[64,8,4]{2,1,0:T(8,128)S(1)} %get-tuple-element.26), kind=kOutput, calls=%fused_computation.26 | convolution fusion | flops 6438912 | bytes 573440 | tf_op jit(solution)/shard_map/ahqk,kahd->qahd/dot_general | solution.py:79
  136.7 0.3 convert_element_type.117
  137.0 6.4 %all_to_all.31 = bf16[1,1,4,1,64,512]{5,4,3,1,0,2:T(8,128)(2,1)S(1)} all-to-all(bf16[1,1,4,1,64,512]{5,4,3,1,0,2:T(8,128)(2,1)S(1)} %bitcast.126), channel_id=1, replica_groups=mesh['gx'=4,'gy'=4,'ta'=2] {'ta'}, dimensions={2} | all-to-all | bytes 524288 | tf_op jit(solution)/shard_map/all_to_all | solution.py:133
  143.4 1.4 fusion.81
  145.1 3.6 %fusion.18 = bf16[1,1,2,128,512]{4,3,2,1,0:T(8,128)(2,1)} fusion(f32[1,1,2,128,512]{4,3,2,1,0:T(8,128)S(1)} %get-tuple-element.29, bf16[2048,512]{1,0:T(8,128)(2,1)S(1)} %copy-done, bf16[512,2048]{1,0:T(8,128)(2,1)} %param.22, f32[512]{0:T(512)S(1)} %bitcast.133, f32[2,128]{1,0:T(2,128)S(1)} %add_rsqrt_fusion, f32[2,128]{1,0:T(2,128)S(1)} %broadcast_multiply_fusion.2), kind=kOutput, calls=%fused_computation.33 | convolution fusion | flops 1075576832 | bytes 4984832 | tf_op jit(solution)/shard_map/dot_general | solution.py:36
  (51 shorter events, 1.3 us)
Async XLA Ops:
  0.0 145.1 %copy-start = (bf16[2048,512]{1,0:T(8,128)(2,1)S(1)}, bf16[2048,512]{1,0:T(8,128)(2,1)}, u32[]{:S(2)}) copy-start(bf16[2048,512]{1,0:T(8,128)(2,1)} %param.23) | copy-start | bytes 6291460
  0.8 6.1 %copy-start.9 = (pred[2,128]{1,0:T(4,128)(4,1)}, pred[2,128]{1,0:T(4,128)(4,1)S(1)}, u32[]{:S(2)}) copy-start(pred[2,128]{1,0:T(4,128)(4,1)S(1)} %compare_bitcast_fusion) | copy-start | bytes 772
  6.8 10.9 %copy-start.7 = (bf16[1,1,2,128,1536]{4,3,2,1,0:T(8,128)(2,1)}, bf16[1,1,2,128,1536]{4,3,2,1,0:T(8,128)(2,1)S(1)}, u32[]{:S(2)}) copy-start(bf16[1,1,2,128,1536]{4,3,2,1,0:T(8,128)(2,1)S(1)} %fusion.1) | copy-start | bytes 2359300
  6.8 23.0 %copy-start.13 = (s32[1,1,9]{2,1,0:T(1,128)S(1)}, s32[1,1,9]{2,1,0:T(1,128)}, u32[]{:S(2)}) copy-start(s32[1,1,9]{2,1,0:T(1,128)} %param.15) | copy-start | bytes 112
  6.9 24.3 %copy-start.11 = (s32[4,4]{1,0:T(4,128)S(1)}, s32[4,4]{1,0:T(4,128)}, u32[]{:S(2)}) copy-start(s32[4,4]{1,0:T(4,128)} %param.14) | copy-start | bytes 196
  6.9 10.8 %collective-permute-start = (bf16[1,1,2,128,1024]{4,3,2,1,0:T(8,128)(2,1)S(1)}, bf16[1,1,2,128,1024]{4,3,2,1,0:T(8,128)(2,1)S(1)}, u32[]{:S(2)}, u32[]{:S(2)}) collective-permute-start(bf16[1,1,2,128,1024]{4,3,2,1,0:T(8,128)(2,1)S(1)} %slice.63), channel_id=1, source_target_pairs={{0,8},{8,16},{16,24},{1,9},{9,17},{17,25},{2,10},{10,18},{18,26},{... | collective-permute-start | bytes 1572872 | tf_op jit(solution)/shard_map/ppermute | solution.py:22
  11.6 10.5 %collective-permute-start.1 = (bf16[1,1,2,128,1024]{4,3,2,1,0:T(8,128)(2,1)S(1)}, bf16[1,1,2,128,1024]{4,3,2,1,0:T(8,128)(2,1)S(1)}, u32[]{:S(2)}, u32[]{:S(2)}) collective-permute-start(bf16[1,1,2,128,1024]{4,3,2,1,0:T(8,128)(2,1)S(1)} %slice.63), channel_id=1, source_target_pairs={{8,0},{16,8},{24,16},{9,1},{17,9},{25,17},{10,2},{18,10},{26,18},{... | collective-permute-start | bytes 1572872 | tf_op jit(solution)/shard_map/ppermute | solution.py:23
  22.1 0.8 copy-start.3
  24.2 31.5 %collective-permute-start.2 = (bf16[3,1,2,128,1024]{4,3,2,1,0:T(8,128)(2,1)}, bf16[3,1,2,128,1024]{4,3,2,1,0:T(8,128)(2,1)}, u32[]{:S(2)}, u32[]{:S(2)}) collective-permute-start(bf16[3,1,2,128,1024]{4,3,2,1,0:T(8,128)(2,1)} %pad_maximum_fusion.1), channel_id=1, source_target_pairs={{0,2},{2,4},{4,6},{1,3},{3,5},{5,7},{8,10},{10,12},{12,14},{9,11},... | collective-permute-start | bytes 4718600 | tf_op jit(solution)/shard_map/ppermute | solution.py:22
  28.5 32.4 %collective-permute-start.3 = (bf16[3,1,2,128,1024]{4,3,2,1,0:T(8,128)(2,1)}, bf16[3,1,2,128,1024]{4,3,2,1,0:T(8,128)(2,1)}, u32[]{:S(2)}, u32[]{:S(2)}) collective-permute-start(bf16[3,1,2,128,1024]{4,3,2,1,0:T(8,128)(2,1)} %pad_maximum_fusion.1), channel_id=1, source_target_pairs={{2,0},{4,2},{6,4},{3,1},{5,3},{7,5},{10,8},{12,10},{14,12},{11,9},... | collective-permute-start | bytes 4718600 | tf_op jit(solution)/shard_map/ppermute | solution.py:23
  74.3 6.3 %copy-start.2 = (bf16[3,3,128,512]{3,2,1,0:T(8,128)(2,1)S(1)}, bf16[3,3,128,512]{3,2,1,0:T(8,128)(2,1)}, u32[]{:S(2)}) copy-start(bf16[3,3,128,512]{3,2,1,0:T(8,128)(2,1)} %get-tuple-element.9) | copy-start | bytes 3538948
  82.9 11.0 %slice-start = ((s8[4718592]{0:T(1024)(128)(4,1)}), s8[524288]{0:T(1024)(128)(4,1)S(1)}, s32[]{:S(2)}) async-start(s8[4718592]{0:T(1024)(128)(4,1)} %bitcast.119), calls=%async_computation.2 | async-start | bytes 1048576
  86.9 7.0 %slice-start.1 = ((s8[4718592]{0:T(1024)(128)(4,1)}), s8[4194304]{0:T(1024)(128)(4,1)S(1)}, s32[]{:S(2)}) async-start(s8[4718592]{0:T(1024)(128)(4,1)} %bitcast.119), calls=%async_computation.3 | async-start | bytes 8388608
  86.9 7.0 %copy-start.5 = (bf16[1152,8,64]{0,2,1:T(8,128)(2,1)S(1)}, bf16[1152,8,64]{0,2,1:T(8,128)(2,1)}, u32[]{:S(2)}) copy-start(bf16[1152,8,64]{0,2,1:T(8,128)(2,1)} %reshape.208) | copy-start | bytes 3538948
  86.9 7.0 %copy-start.10 = (pred[1152]{0:T(1024)(128)(4,1)S(1)}, pred[1152]{0:T(1024)(128)(4,1)}, u32[]{:S(2)}) copy-start(pred[1152]{0:T(1024)(128)(4,1)} %and.17) | copy-start | bytes 3460
  99.5 6.2 %copy-start.1 = (bf16[3,3,128,512]{3,2,1,0:T(8,128)(2,1)S(1)}, bf16[3,3,128,512]{3,2,1,0:T(8,128)(2,1)}, u32[]{:S(2)}) copy-start(bf16[3,3,128,512]{3,2,1,0:T(8,128)(2,1)} %get-tuple-element.30) | copy-start | bytes 3538948
  110.8 5.4 %copy-start.6 = (bf16[1,1,2,128,512]{4,3,2,1,0:T(8,128)(2,1)S(1)}, bf16[1,1,2,128,512]{4,3,2,1,0:T(8,128)(2,1)}, u32[]{:S(2)}) copy-start(bf16[1,1,2,128,512]{4,3,2,1,0:T(8,128)(2,1)} %param.12) | copy-start | bytes 786436
  110.9 5.4 %copy-start.8 = (bf16[512]{0:T(512)(128)(2,1)S(1)}, bf16[512]{0:T(512)(128)(2,1)}, u32[]{:S(2)}) copy-start(bf16[512]{0:T(512)(128)(2,1)} %param.16) | copy-start | bytes 3076
  116.2 1.8 %copy-start.4 = (bf16[512,1536]{1,0:T(8,128)(2,1)S(1)}, bf16[512,1536]{1,0:T(8,128)(2,1)}, u32[]{:S(2)}) copy-start(bf16[512,1536]{1,0:T(8,128)(2,1)} %param.20) | copy-start | bytes 4718596
  136.7 8.4 %copy-start.12 = (f32[1,512]{1,0:T(1,128)S(1)}, f32[1,512]{1,0:T(1,128)}, u32[]{:S(2)}) copy-start(f32[1,512]{1,0:T(1,128)} %get-tuple-element.18) | copy-start | bytes 6148
where the time goes:
time: 150 us; the launch traced here: 149 us
  local copies, waits for them, and re-layouts  39.4 us (26%)
  waiting for transfers between devices  37.5 us (25%)
  matrix products  32 us (21%)
  blocking collectives  15.7 us (10%)
  starting transfers between devices  12.2 us (8%)
  other arithmetic  11.6 us (8%)
    ppermute x2, waiting for transfers between devices, extended(): before = lax.ppermute(last, axis, up)  27.9 us
    mul x2, local copies, waits for them, and re-layouts, agent_block(): scores.reshape(head_count, slot_count, 9 * slot_count)  12.5 us
    dot_general x2, matrix products, agent_block(): jnp.einsum('qhd,xykhd->hqxyk', own_queries, key_rows, preferred_element_t...  11.7 us
    ppermute x2, waiting for transfers between devices, extended(): after = lax.ppermute(first, axis, down)  9.63 us
    dot_general x5, matrix products, project(): return jnp.dot(values, weight, preferred_element_type=jnp.float32)  9.4 us
    all_to_all x1, blocking collectives, per_device(): lax.all_to_all(grouped, 'ta', split_axis=3, concat_axis=2, tiled=True)  9.27 us
    ppermute x2, starting transfers between devices, extended(): before = lax.ppermute(last, axis, up)  8.99 us
    reshape x2, local copies, waits for them, and re-layouts, agent_block(): beside_all[..., model_width:].reshape(9 * slot_count, head_count, head_dim)  6.82 us
  transfers between devices with their start and end apart: 4, of which 4 were waited for; matrix products, arithmetic and copies ran while one was open for 1% of the time, Pallas kernels for 0%

commit v1 on v0

v1 whole, which is shorter than its diff:
```python
import functools

import jax
import jax.numpy as jnp
from jax import lax
from jax.experimental import pallas as pl
from jax.experimental.pallas import tpu as pltpu
from jax.sharding import PartitionSpec as P

HEADS = 8
EPSILON = 1e-05
NEGATIVE = -1e30
F32 = jnp.float32
BF16 = jnp.bfloat16
MESH = pl.DeviceIdType.MESH

OFFSETS = ((0, 0), (-1, 0), (1, 0), (0, -1), (0, 1), (-1, -1), (1, -1), (-1, 1), (1, 1))


def layer_norm(values, gain_row):
    values = values.astype(F32)
    center = values - jnp.mean(values, axis=-1, keepdims=True)
    spread = jnp.mean(center * center, axis=-1, keepdims=True)
    return (center * lax.rsqrt(spread + EPSILON) * gain_row).astype(BF16)


def dot(a, b):
    return jnp.dot(a, b, preferred_element_type=F32)


def dot_t(a, b):
    return lax.dot_general(a, b, (((1,), (1,)), ((), ())), preferred_element_type=F32)


def kernel(
    sizes,
    tokens,
    validity,
    counts,
    flags,
    mask_token,
    gains,
    *rest,
):
    nx, ny, nt = sizes
    weights_hbm = rest[:6]
    out = rest[6]
    weights = rest[7:13]
    (tok, near, masked, query, kv, after, steps, tq, tkv, tmix) = rest[13:23]
    (load_sem, send_sem, recv_sem, tsend_sem, trecv_sem) = rest[23:]
    moments, slots, width = tok.shape
    head_dim = width // HEADS
    scale = head_dim**-0.5
    gx, gy, ta = lax.axis_index("gx"), lax.axis_index("gy"), lax.axis_index("ta")
    has = {-1: gx > 0, 1: gx < nx - 1}
    hasy = {-1: gy > 0, 1: gy < ny - 1}

    def load(i, src, dst):
        return pltpu.make_async_copy(src, dst, load_sem.at[i])

    loads = [load(0, tokens, tok)] + [
        load(i + 1, s, d) for i, (s, d) in enumerate(zip(weights_hbm, weights))
    ]
    for item in loads:
        item.start()

    barrier = pltpu.get_barrier_semaphore()
    for d in (-1, 1):

        @pl.when(has[d])
        def _():
            pl.semaphore_signal(barrier, inc=1, device_id=(gx + d, gy, ta), device_id_type=MESH)

        @pl.when(hasy[d])
        def _():
            pl.semaphore_signal(barrier, inc=1, device_id=(gx, gy + d, ta), device_id_type=MESH)

    for k in range(1, nt):
        pl.semaphore_signal(
            barrier, inc=1, device_id=(gx, gy, lax.rem(ta + k, nt)), device_id_type=MESH
        )

    for index, (di, dj) in enumerate(OFFSETS):
        inside = None
        for d, table in ((di, has), (dj, hasy)):
            if d:
                inside = table[d] if inside is None else jnp.logical_and(inside, table[d])
        if inside is not None:

            @pl.when(jnp.logical_not(inside))
            def _():
                near[index] = jnp.zeros(near.shape[1:], BF16)

    def along_y(m, d):
        dst = OFFSETS.index((0, -d))
        return pltpu.make_async_remote_copy(
            near.at[0, m], near.at[dst, m], send_sem.at[dst, m], recv_sem.at[dst, m],
            device_id=(gx, gy + d, ta), device_id_type=MESH,
        )

    def along_x(m, d, dj):
        src, dst = OFFSETS.index((0, dj)), OFFSETS.index((-d, dj))
        return pltpu.make_async_remote_copy(
            near.at[src, m], near.at[dst, m], send_sem.at[dst, m], recv_sem.at[dst, m],
            device_id=(gx + d, gy, ta), device_id_type=MESH,
        )

    def along_t(m, k):
        return pltpu.make_async_remote_copy(
            steps.at[m], steps.at[k * moments + m], tsend_sem.at[k - 1, m], trecv_sem.at[k - 1, m],
            device_id=(gx, gy, lax.rem(ta + k, nt)), device_id_type=MESH,
        )

    loads[0].wait()
    greeted = (nt - 1) + sum(
        jnp.where(c, 1, 0).astype(jnp.int32) for c in (has[-1], has[1], hasy[-1], hasy[1])
    )
    for m in range(moments):
        seen = jnp.broadcast_to(validity[m : m + 1, :].astype(F32), (128, slots)).T
        seen = jnp.concatenate([seen] * (width // 128), axis=1) == 1.0
        x = jnp.where(seen, tok[m].astype(F32), mask_token[...].astype(F32))
        masked[m] = x.astype(BF16)
        near[0, m] = layer_norm(x, gains[0:1, :])
        if m == 0:
            pl.semaphore_wait(barrier, greeted)
        for d in (-1, 1):

            @pl.when(hasy[d])
            def _():
                along_y(m, d).start()

        for d in (-1, 1):

            @pl.when(has[d])
            def _():
                along_x(m, d, 0).start()

    qkv_w, out_w, tqkv_w, tout_w, widen_w, narrow_w = weights
    loads[1].wait()
    own = near[0].reshape(moments * slots, width)
    query[...] = (dot(own, qkv_w[:, :width]) * scale).astype(BF16).reshape(query.shape)
    own_kv = dot(own, qkv_w[:, width:]).astype(BF16)
    for m in range(moments):
        kv[m, :slots] = own_kv[m * slots : (m + 1) * slots]

    def project_near(m, first, last):
        rows = near[first:last, m].reshape((last - first) * slots, width)
        kv[m, first * slots : last * slots] = dot(rows, qkv_w[:, width:]).astype(BF16)

    for m in range(moments):
        for dj in (-1, 1):

            @pl.when(hasy[dj])
            def _():
                along_y(m, -dj).wait_recv()
                for d in (-1, 1):

                    @pl.when(has[d])
                    def _():
                        along_x(m, d, dj).start()

        for d in (-1, 1):

            @pl.when(has[d])
            def _():
                along_x(m, -d, 0).wait_recv()

        project_near(m, 1, 5)

    lane = lax.broadcasted_iota(jnp.int32, (1, slots), 1)
    live = []
    for di, dj in OFFSETS:
        i, j = gx + di, gy + dj
        inside = jnp.logical_and(
            jnp.logical_and(i >= 0, i < nx), jnp.logical_and(j >= 0, j < ny)
        )
        count = counts[jnp.clip(i, 0, nx - 1), jnp.clip(j, 0, ny - 1)]
        chosen = flags[0, 3 * (di + 1) + (dj + 1)] == 1
        limit = jnp.where(jnp.logical_and(inside, chosen), count, 0)
        live.append(jnp.where(lane < limit, 0.0, 1.0))
    live = jnp.concatenate(live, axis=1) == 0.0

    group = 256
    heads_in = group // head_dim
    head_of = lax.broadcasted_iota(jnp.int32, (slots, group), 1) // head_dim

    loads[2].wait()
    for m in range(moments):
        for d in (-1, 1):
            for dj in (-1, 1):

                @pl.when(jnp.logical_and(has[d], hasy[dj]))
                def _():
                    along_x(m, -d, dj).wait_recv()

        project_near(m, 5, 9)
        parts = []
        for g in range(width // group):
            q = query[m, :, g * group : (g + 1) * group]
            stacked = jnp.concatenate(
                [jnp.where(head_of == h, q, jnp.zeros_like(q)) for h in range(heads_in)], axis=0
            )
            keys = kv[m, :, g * group : (g + 1) * group]
            values = kv[m, :, width + g * group : width + (g + 1) * group]
            scores = jnp.where(live, dot_t(stacked, keys), NEGATIVE)
            top = jnp.max(scores, axis=-1, keepdims=True)
            soft = jnp.exp(scores - top)
            total = jnp.sum(soft, axis=-1, keepdims=True)
            mixed = dot(soft.astype(BF16), values) * (1.0 / total)
            part = mixed[:slots]
            for h in range(1, heads_in):
                part = jnp.where(head_of == h, mixed[h * slots : (h + 1) * slots], part)
            parts.append(part.astype(BF16))
        mix = jnp.concatenate(parts, axis=1)
        result = (masked[m].astype(F32) + dot(mix, out_w[...])).astype(BF16)
        after[m] = result
        steps[m] = layer_norm(result, gains[1:2, :])
        for k in range(1, nt):
            along_t(m, k).start()

    loads[3].wait()
    rows = steps[:moments].reshape(moments * slots, width)
    tq[...] = (dot(rows, tqkv_w[:, :width]) * scale).astype(BF16).reshape(tq.shape)
    tkv[:moments] = (
        dot(rows, tqkv_w[:, width:]).astype(BF16).reshape(moments, slots, 2 * width)
    )
    for k in range(1, nt):
        for m in range(moments):
            along_t(m, k).wait_recv()
        rows = steps[k * moments : (k + 1) * moments].reshape(moments * slots, width)
        tkv[k * moments : (k + 1) * moments] = (
            dot(rows, tqkv_w[:, width:]).astype(BF16).reshape(moments, slots, 2 * width)
        )

    total_steps = nt * moments
    same = (
        lax.broadcasted_iota(jnp.int32, (group, group), 0) // head_dim
        == lax.broadcasted_iota(jnp.int32, (group, group), 1) // head_dim
    )
    ones = jnp.where(same, 1.0, 0.0).astype(BF16)
    piece = max(16, min(slots, 512 // total_steps))

    def time_piece(start):
        at = pl.ds(start, piece)
        for m in range(moments):
            for g in range(width // group):
                cols = slice(g * group, (g + 1) * group)
                q = tq[m, at, cols].astype(F32)
                keys = tkv[:, at, cols].astype(F32)
                prod = (q[None] * keys).reshape(total_steps * piece, group)
                high = prod.astype(BF16)
                low = (prod - high.astype(F32)).astype(BF16)
                scores = (dot(high, ones) + dot(low, ones)).reshape(total_steps, piece, group)
                soft = jnp.exp(scores - jnp.max(scores, axis=0)[None])
                total = jnp.sum(soft, axis=0)
                values = tkv[:, at, width + g * group : width + (g + 1) * group].astype(F32)
                mixed = jnp.sum(soft * values, axis=0) / total
                tmix[m, at, cols] = mixed.astype(BF16)

    if piece == slots:
        time_piece(0)
    else:

        def body(i, carry):
            time_piece(pl.multiple_of(i * piece, piece))
            return carry

        lax.fori_loop(0, slots // piece, body, 0)

    loads[4].wait()
    rows = moments * slots
    after_time = (
        after[...].reshape(rows, width).astype(F32)
        + dot(tmix[...].reshape(rows, width), tout_w[...])
    ).astype(BF16)
    normed = layer_norm(after_time, gains[2:3, :])
    loads[5].wait()
    hidden = jnp.maximum(dot(normed, widen_w[...]), 0.0).astype(BF16)
    loads[6].wait()
    out[...] = (
        (after_time.astype(F32) + dot(hidden, narrow_w[...])).astype(BF16).reshape(out.shape)
    )

    for m in range(moments):
        for d in (-1, 1):

            @pl.when(hasy[d])
            def _():
                along_y(m, d).wait_send()

            @pl.when(has[d])
            def _():
                along_x(m, d, 0).wait_send()

            for dj in (-1, 1):

                @pl.when(jnp.logical_and(has[d], hasy[dj]))
                def _():
                    along_x(m, d, dj).wait_send()

        for k in range(1, nt):
            along_t(m, k).wait_send()


def per_device(sizes, tokens, validity, tile_counts, neighbours, mask_token, norm_gains, *weights):
    moments, slots, width = tokens.shape[2:]
    steps = moments * sizes[2]
    vmem = pl.BlockSpec(memory_space=pltpu.VMEM)
    smem = pl.BlockSpec(memory_space=pltpu.SMEM)
    anywhere = pl.BlockSpec(memory_space=pl.ANY)
    result = pl.pallas_call(
        functools.partial(kernel, sizes),
        out_shape=jax.ShapeDtypeStruct((moments, slots, width), BF16),
        in_specs=[anywhere, vmem, smem, smem, vmem, vmem] + [anywhere] * 6,
        out_specs=vmem,
        scratch_shapes=[pltpu.VMEM(w.shape, BF16) for w in weights]
        + [
            pltpu.VMEM((moments, slots, width), BF16),
            pltpu.VMEM((9, moments, slots, width), BF16),
            pltpu.VMEM((moments, slots, width), BF16),
            pltpu.VMEM((moments, slots, width), BF16),
            pltpu.VMEM((moments, 9 * slots, 2 * width), BF16),
            pltpu.VMEM((moments, slots, width), BF16),
            pltpu.VMEM((steps, slots, width), BF16),
            pltpu.VMEM((moments, slots, width), BF16),
            pltpu.VMEM((steps, slots, 2 * width), BF16),
            pltpu.VMEM((moments, slots, width), BF16),
            pltpu.SemaphoreType.DMA((7,)),
            pltpu.SemaphoreType.DMA((9, moments)),
            pltpu.SemaphoreType.DMA((9, moments)),
            pltpu.SemaphoreType.DMA((max(sizes[2] - 1, 1), moments)),
            pltpu.SemaphoreType.DMA((max(sizes[2] - 1, 1), moments)),
        ],
        compiler_params=pltpu.CompilerParams(
            collective_id=0, has_side_effects=True, vmem_limit_bytes=56 * 1024 * 1024
        ),
    )(
        tokens[0, 0],
        validity[0, 0],
        tile_counts,
        neighbours[0],
        mask_token[None],
        norm_gains,
        *weights,
    )
    return result[None, None]


def solution(mesh):
    sizes = tuple(mesh.shape[name] for name in ("gx", "gy", "ta"))
    in_specs = (
        P("gx", "gy", "ta", None, None),
        P("gx", "gy", "ta", None),
        P(),
        P("gx", "gy", None),
    ) + (P(),) * 8
    return jax.shard_map(
        functools.partial(per_device, sizes),
        mesh=mesh,
        in_specs=in_specs,
        out_specs=P("gx", "gy", "ta", None, None),
        check_vma=False,
    )
```

time: 150 us -> 32.5 us (0.22)
  the two profiles are of different devices: /device:TPU:1 before, /device:TPU:0 now
where the time goes in v1:
time: 32.5 us; the launch traced here: 32.2 us
  Pallas kernels  29.3 us (90%)
  local copies, waits for them, and re-layouts  2.93 us (9%)
    pallas_call x1, Pallas kernels, per_device(): pl.pallas_call(functools.partial(kernel, sizes), out_shape=jax.ShapeDtype...  29.3 us
    unnamed x1, local copies, waits for them, and re-layouts  1.67 us
    broadcast_in_dim x1, local copies, waits for them, and re-layouts, per_device(): mask_token[None]  1.26 us

profile of v1, /device:TPU:0, one launch (start us, length us, event | category | flops | bytes accessed | tf_op | source)
XLA Modules:
  0.0 32.2 jit_solution(5208367700035827649)
XLA Ops:
  0.0 1.3 %broadcast_in_dim.6.mask_token = bf16[1,512]{1,0:T(2,128)(2,1)} reshape(bf16[512]{0:T(512)(128)(2,1)} %param.16) | data formatting | bytes 2048 | tf_op jit(solution)/shard_map/broadcast_in_dim | solution.py:342
  1.3 29.3 %shard_map.118 = bf16[2,128,512]{2,1,0:T(8,128)(2,1)} custom-call(bf16[2,128,512]{2,1,0:T(8,128)(2,1)} %bitcast.5, s32[2,128]{1,0:T(2,128)} %bitcast.6, s32[4,4]{1,0:T(4,128)} %counts.1, s32[1,9]{1,0:T(1,128)} %bitcast.7, bf16[1,512]{1,0:T(2,128)(2,1)} %broadcast_in_dim.6.mask_token, f32[3,512]{1,0:T(4,128)} %gains.1, bf16[512,1536]{1,0:T(8,128)(2,1)} %rest_0_.1, ...), custom_call_target="tpu_custom_call" | custom-call | tf_op jit(solution)/shard_map/pallas_call | solution.py:311
  30.6 1.7 %copy.14 = bf16[1,1,2,128,512]{4,3,2,1,0:T(8,128)(2,1)} copy(bf16[1,1,2,128,512]{4,3,2,1,0:T(8,128)(2,1)} %bitcast.4) | data formatting | bytes 524288

commit v2 on v1

--- a/solution.py
+++ b/solution.py
@@ -46,8 +46,8 @@
     weights_hbm = rest[:6]
     out = rest[6]
     weights = rest[7:13]
-    (tok, near, masked, query, kv, after, steps, tq, tkv, tmix) = rest[13:23]
-    (load_sem, send_sem, recv_sem, tsend_sem, trecv_sem) = rest[23:]
+    (tok, near, masked, query, kv, after, steps, tq, tkv, tmix, held) = rest[13:24]
+    (load_sem, send_sem, recv_sem, tsend_sem, trecv_sem) = rest[24:]
     moments, slots, width = tok.shape
     head_dim = width // HEADS
     scale = head_dim**-0.5
@@ -111,6 +111,7 @@
             device_id=(gx, gy, lax.rem(ta + k, nt)), device_id_type=MESH,
         )
 
+    hidden_token = mask_token[...].astype(F32)[None, :]
     loads[0].wait()
     greeted = (nt - 1) + sum(
         jnp.where(c, 1, 0).astype(jnp.int32) for c in (has[-1], has[1], hasy[-1], hasy[1])
@@ -118,7 +119,7 @@
     for m in range(moments):
         seen = jnp.broadcast_to(validity[m : m + 1, :].astype(F32), (128, slots)).T
         seen = jnp.concatenate([seen] * (width // 128), axis=1) == 1.0
-        x = jnp.where(seen, tok[m].astype(F32), mask_token[...].astype(F32))
+        x = jnp.where(seen, tok[m].astype(F32), hidden_token)
         masked[m] = x.astype(BF16)
         near[0, m] = layer_norm(x, gains[0:1, :])
         if m == 0:
@@ -146,26 +147,6 @@
     def project_near(m, first, last):
         rows = near[first:last, m].reshape((last - first) * slots, width)
         kv[m, first * slots : last * slots] = dot(rows, qkv_w[:, width:]).astype(BF16)
-
-    for m in range(moments):
-        for dj in (-1, 1):
-
-            @pl.when(hasy[dj])
-            def _():
-                along_y(m, -dj).wait_recv()
-                for d in (-1, 1):
-
-                    @pl.when(has[d])
-                    def _():
-                        along_x(m, d, dj).start()
-
-        for d in (-1, 1):
-
-            @pl.when(has[d])
-            def _():
-                along_x(m, -d, 0).wait_recv()
-
-        project_near(m, 1, 5)
 
     lane = lax.broadcasted_iota(jnp.int32, (1, slots), 1)
     live = []
@@ -184,34 +165,89 @@
     heads_in = group // head_dim
     head_of = lax.broadcasted_iota(jnp.int32, (slots, group), 1) // head_dim
 
-    loads[2].wait()
-    for m in range(moments):
-        for d in (-1, 1):
-            for dj in (-1, 1):
-
-                @pl.when(jnp.logical_and(has[d], hasy[dj]))
-                def _():
-                    along_x(m, -d, dj).wait_recv()
-
-        project_near(m, 5, 9)
+
+    def merge(first, second):
+        acc_a, top_a, sum_a = first
+        acc_b, top_b, sum_b = second
+        top = jnp.maximum(top_a, top_b)
+        a, b = jnp.exp(top_a - top), jnp.exp(top_b - top)
+        return acc_a * a + acc_b * b, top, sum_a * a + sum_b * b
+
+    def attend(m, first, last):
         parts = []
+        span = slice(first * slots, last * slots)
         for g in range(width // group):
             q = query[m, :, g * group : (g + 1) * group]
             stacked = jnp.concatenate(
                 [jnp.where(head_of == h, q, jnp.zeros_like(q)) for h in range(heads_in)], axis=0
             )
-            keys = kv[m, :, g * group : (g + 1) * group]
-            values = kv[m, :, width + g * group : width + (g + 1) * group]
-            scores = jnp.where(live, dot_t(stacked, keys), NEGATIVE)
+            keys = kv[m, span, g * group : (g + 1) * group]
+            values = kv[m, span, width + g * group : width + (g + 1) * group]
+            scores = jnp.where(live[:, span], dot_t(stacked, keys), NEGATIVE)
             top = jnp.max(scores, axis=-1, keepdims=True)
             soft = jnp.exp(scores - top)
             total = jnp.sum(soft, axis=-1, keepdims=True)
-            mixed = dot(soft.astype(BF16), values) * (1.0 / total)
-            part = mixed[:slots]
-            for h in range(1, heads_in):
-                part = jnp.where(head_of == h, mixed[h * slots : (h + 1) * slots], part)
-            parts.append(part.astype(BF16))
-        mix = jnp.concatenate(parts, axis=1)
+            mixed = dot(soft.astype(BF16), values)
+
+            def pick(rows):
+                part = jnp.broadcast_to(rows[:slots], (slots, group))
+                for h in range(1, heads_in):
+                    part = jnp.where(head_of == h, rows[h * slots : (h + 1) * slots], part)
+                return part
+
+            parts.append([pick(mixed), pick(top), pick(total)])
+        return [jnp.concatenate(p, axis=1) for p in zip(*parts)]
+
+    def keep(m, state):
+        for n in range(3):
+            held[m, n] = state[n]
+
+    def kept(m):
+        return [held[m, n] for n in range(3)]
+
+    def first_part(m):
+        keep(m, attend(m, 0, 3))
+
+    def second_part(m):
+        project_near(m, 3, 5)
+        keep(m, merge(kept(m), attend(m, 3, 5)))
+
+    for m in range(moments):
+        for d in (-1, 1):
+
+            @pl.when(has[d])
+            def _():
+                along_x(m, -d, 0).wait_recv()
+
+        project_near(m, 1, 3)
+        for dj in (-1, 1):
+
+            @pl.when(hasy[dj])
+            def _():
+                along_y(m, -dj).wait_recv()
+                for d in (-1, 1):
+
+                    @pl.when(has[d])
+                    def _():
+                        along_x(m, d, dj).start()
+
+        if m > 0:
+            second_part(m - 1)
+        first_part(m)
+    second_part(moments - 1)
+
+    loads[2].wait()
+    for m in range(moments):
+        for d in (-1, 1):
+            for dj in (-1, 1):
+
+                @pl.when(jnp.logical_and(has[d], hasy[dj]))
+                def _():
+                    along_x(m, -d, dj).wait_recv()
+
+        project_near(m, 5, 9)
+        acc, _, total = merge(kept(m), attend(m, 5, 9))
+        mix = (acc / total).astype(BF16)
         result = (masked[m].astype(F32) + dot(mix, out_w[...])).astype(BF16)
         after[m] = result
         steps[m] = layer_norm(result, gains[1:2, :])
@@ -224,13 +260,10 @@
     tkv[:moments] = (
         dot(rows, tqkv_w[:, width:]).astype(BF16).reshape(moments, slots, 2 * width)
     )
-    for k in range(1, nt):
-        for m in range(moments):
+    for m in range(moments):
+        for k in range(1, nt):
             along_t(m, k).wait_recv()
-        rows = steps[k * moments : (k + 1) * moments].reshape(moments * slots, width)
-        tkv[k * moments : (k + 1) * moments] = (
-            dot(rows, tqkv_w[:, width:]).astype(BF16).reshape(moments, slots, 2 * width)
-        )
+            tkv[k * moments + m] = dot(steps[k * moments + m], tqkv_w[:, width:]).astype(BF16)
 
     total_steps = nt * moments
     same = (
@@ -325,6 +358,7 @@
             pltpu.VMEM((moments, slots, width), BF16),
             pltpu.VMEM((steps, slots, 2 * width), BF16),
             pltpu.VMEM((moments, slots, width), BF16),
+            pltpu.VMEM((moments, 3, slots, width), F32),
             pltpu.SemaphoreType.DMA((7,)),
             pltpu.SemaphoreType.DMA((9, moments)),
             pltpu.SemaphoreType.DMA((9, moments)),
@@ -339,7 +373,7 @@
         validity[0, 0],
         tile_counts,
         neighbours[0],
-        mask_token[None],
+        mask_token,
         norm_gains,
         *weights,
     )

time: 32.5 us -> 30.3 us (0.932)
  local copies, waits for them, and re-layouts: 2.93 us -> 1.67 us
  Pallas kernels: 29.3 us -> 28.5 us
    broadcast_in_dim x1 -> x0, local copies, waits for them, and re-layouts: 1.26 us -> none  [per_device(): mask_token[None]]
    pallas_call x1, Pallas kernels: 29.3 us -> 28.5 us  [per_device(): pl.pallas_call(functools.partial(kernel, sizes), out_shape=jax.ShapeDtype...]
where the time goes in v2:
time: 30.3 us; the launch traced here: 30.1 us
  Pallas kernels  28.5 us (94%)
  local copies, waits for them, and re-layouts  1.67 us (6%)
    pallas_call x1, Pallas kernels, per_device(): pl.pallas_call(functools.partial(kernel, sizes), out_shape=jax.ShapeDtype...  28.5 us
    unnamed x1, local copies, waits for them, and re-layouts  1.67 us

profile of v2, /device:TPU:0, one launch (start us, length us, event | category | flops | bytes accessed | tf_op | source)
XLA Modules:
  0.0 30.1 jit_solution(2662994584580953641)
XLA Ops:
  0.0 28.5 %shard_map.118 = bf16[2,128,512]{2,1,0:T(8,128)(2,1)} custom-call(bf16[2,128,512]{2,1,0:T(8,128)(2,1)} %bitcast.5, s32[2,128]{1,0:T(2,128)} %bitcast.6, s32[4,4]{1,0:T(4,128)} %counts.1, s32[1,9]{1,0:T(1,128)} %bitcast.7, bf16[512]{0:T(512)(128)(2,1)} %mask_token.1, f32[3,512]{1,0:T(4,128)} %gains.1, bf16[512,1536]{1,0:T(8,128)(2,1)} %rest_0_.1, ...), custom_call_target="tpu_custom_call" | custom-call | tf_op jit(solution)/shard_map/pallas_call | solution.py:344
  28.5 1.7 %copy.14 = bf16[1,1,2,128,512]{4,3,2,1,0:T(8,128)(2,1)} copy(bf16[1,1,2,128,512]{4,3,2,1,0:T(8,128)(2,1)} %bitcast.4) | data formatting | bytes 524288

commit v3 on v2

--- a/solution.py
+++ b/solution.py
@@ -10,6 +10,7 @@
 HEADS = 8
 EPSILON = 1e-05
 NEGATIVE = -1e30
+CUTS = 2
 F32 = jnp.float32
 BF16 = jnp.bfloat16
 MESH = pl.DeviceIdType.MESH
@@ -51,6 +52,7 @@
     moments, slots, width = tok.shape
     head_dim = width // HEADS
     scale = head_dim**-0.5
+    cuts = CUTS
     gx, gy, ta = lax.axis_index("gx"), lax.axis_index("gy"), lax.axis_index("ta")
     has = {-1: gx > 0, 1: gx < nx - 1}
     hasy = {-1: gy > 0, 1: gy < ny - 1}
@@ -105,9 +107,11 @@
             device_id=(gx + d, gy, ta), device_id_type=MESH,
         )
 
-    def along_t(m, k):
+    def along_t(m, k, c):
+        at = pl.ds(c * slots // cuts, slots // cuts)
         return pltpu.make_async_remote_copy(
-            steps.at[m], steps.at[k * moments + m], tsend_sem.at[k - 1, m], trecv_sem.at[k - 1, m],
+            steps.at[m, at], steps.at[k * moments + m, at],
+            tsend_sem.at[k - 1, m * cuts + c], trecv_sem.at[k - 1, m * cuts + c],
             device_id=(gx, gy, lax.rem(ta + k, nt)), device_id_type=MESH,
         )
 
@@ -173,13 +177,16 @@
         a, b = jnp.exp(top_a - top), jnp.exp(top_b - top)
         return acc_a * a + acc_b * b, top, sum_a * a + sum_b * b
 
-    def attend(m, first, last):
+    def attend(m, first, last, low=0, high=None):
+        high = slots if high is None else high
+        count = high - low
+        lanes = head_of[:count]
         parts = []
         span = slice(first * slots, last * slots)
         for g in range(width // group):
-            q = query[m, :, g * group : (g + 1) * group]
+            q = query[m, low:high, g * group : (g + 1) * group]
             stacked = jnp.concatenate(
-                [jnp.where(head_of == h, q, jnp.zeros_like(q)) for h in range(heads_in)], axis=0
+                [jnp.where(lanes == h, q, jnp.zeros_like(q)) for h in range(heads_in)], axis=0
             )
             keys = kv[m, span, g * group : (g + 1) * group]
             values = kv[m, span, width + g * group : width + (g + 1) * group]
@@ -190,9 +197,9 @@
             mixed = dot(soft.astype(BF16), values)
 
             def pick(rows):
-                part = jnp.broadcast_to(rows[:slots], (slots, group))
+                part = jnp.broadcast_to(rows[:count], (count, group))
                 for h in range(1, heads_in):
-                    part = jnp.where(head_of == h, rows[h * slots : (h + 1) * slots], part)
+                    part = jnp.where(lanes == h, rows[h * count : (h + 1) * count], part)
                 return part
 
             parts.append([pick(mixed), pick(top), pick(total)])
@@ -220,6 +227,8 @@
                 along_x(m, -d, 0).wait_recv()
 
         project_near(m, 1, 3)
+        if m == 0:
+            first_part(m)
         for dj in (-1, 1):
 
             @pl.when(hasy[dj])
@@ -233,7 +242,7 @@
 
         if m > 0:
             second_part(m - 1)
-        first_part(m)
+            first_part(m)
     second_part(moments - 1)
 
     loads[2].wait()
@@ -246,13 +255,16 @@
                     along_x(m, -d, dj).wait_recv()
 
         project_near(m, 5, 9)
-        acc, _, total = merge(kept(m), attend(m, 5, 9))
-        mix = (acc / total).astype(BF16)
-        result = (masked[m].astype(F32) + dot(mix, out_w[...])).astype(BF16)
-        after[m] = result
-        steps[m] = layer_norm(result, gains[1:2, :])
-        for k in range(1, nt):
-            along_t(m, k).start()
+        for c in range(cuts):
+            at = slice(c * slots // cuts, (c + 1) * slots // cuts)
+            state = [held[m, n, at] for n in range(3)]
+            acc, _, total = merge(state, attend(m, 5, 9, at.start, at.stop))
+            mix = (acc / total).astype(BF16)
+            result = (masked[m, at].astype(F32) + dot(mix, out_w[...])).astype(BF16)
+            after[m, at] = result
+            steps[m, at] = layer_norm(result, gains[1:2, :])
+            for k in range(1, nt):
+                along_t(m, k, c).start()
 
     loads[3].wait()
     rows = steps[:moments].reshape(moments * slots, width)
@@ -262,7 +274,8 @@
     )
     for m in range(moments):
         for k in range(1, nt):
-            along_t(m, k).wait_recv()
+            for c in range(cuts):
+                along_t(m, k, c).wait_recv()
             tkv[k * moments + m] = dot(steps[k * moments + m], tqkv_w[:, width:]).astype(BF16)
 
     total_steps = nt * moments
@@ -332,7 +345,8 @@
                     along_x(m, d, dj).wait_send()
 
         for k in range(1, nt):
-            along_t(m, k).wait_send()
+            for c in range(cuts):
+                along_t(m, k, c).wait_send()
 
 
 def per_device(sizes, tokens, validity, tile_counts, neighbours, mask_token, norm_gains, *weights):
@@ -362,8 +376,8 @@
             pltpu.SemaphoreType.DMA((7,)),
             pltpu.SemaphoreType.DMA((9, moments)),
             pltpu.SemaphoreType.DMA((9, moments)),
-            pltpu.SemaphoreType.DMA((max(sizes[2] - 1, 1), moments)),
-            pltpu.SemaphoreType.DMA((max(sizes[2] - 1, 1), moments)),
+            pltpu.SemaphoreType.DMA((max(sizes[2] - 1, 1), moments * CUTS)),
+            pltpu.SemaphoreType.DMA((max(sizes[2] - 1, 1), moments * CUTS)),
         ],
         compiler_params=pltpu.CompilerParams(
             collective_id=0, has_side_effects=True, vmem_limit_bytes=56 * 1024 * 1024

time: 30.3 us -> 30.3 us (level)
  no operation moved by 1% of the time
where the time goes in v3:
time: 30.3 us; the launch traced here: 30.2 us
  Pallas kernels  28.5 us (94%)
  local copies, waits for them, and re-layouts  1.67 us (6%)
    pallas_call x1, Pallas kernels, per_device(): pl.pallas_call(functools.partial(kernel, sizes), out_shape=jax.ShapeDtype...  28.5 us
    unnamed x1, local copies, waits for them, and re-layouts  1.67 us

profile of v3, /device:TPU:0, one launch (start us, length us, event | category | flops | bytes accessed | tf_op | source)
XLA Modules:
  0.0 30.2 jit_solution(1127154538651660979)
XLA Ops:
  0.0 28.5 %shard_map.118 = bf16[2,128,512]{2,1,0:T(8,128)(2,1)} custom-call(bf16[2,128,512]{2,1,0:T(8,128)(2,1)} %bitcast.5, s32[2,128]{1,0:T(2,128)} %bitcast.6, s32[4,4]{1,0:T(4,128)} %counts.1, s32[1,9]{1,0:T(1,128)} %bitcast.7, bf16[512]{0:T(512)(128)(2,1)} %mask_token.1, f32[3,512]{1,0:T(4,128)} %gains.1, bf16[512,1536]{1,0:T(8,128)(2,1)} %rest_0_.1, ...), custom_call_target="tpu_custom_call" | custom-call | tf_op jit(solution)/shard_map/pallas_call | solution.py:358
  28.5 1.7 %copy.14 = bf16[1,1,2,128,512]{4,3,2,1,0:T(8,128)(2,1)} copy(bf16[1,1,2,128,512]{4,3,2,1,0:T(8,128)(2,1)} %bitcast.4) | data formatting | bytes 524288
